TPU v7x, 256 devices: a whole 4x4x8 slice. The times are simulated.
256 devices in a mesh: grp: 4 (over x_hi, core), blk: 64 (over y, x_lo, z).
Axes of the slice: x: 4 (x_hi: 2, x_lo: 2; x = x_hi * 2 + x_lo), y: 4, z: 8, core: 2. Of those that a mesh axis runs over, the one named last changes fastest.
Arguments:
- picture_tower_mean: bfloat16 [8192, 6144], P('blk', 'grp'), may hold values from -6 to 6
- caption_tower_mean: bfloat16 [8192, 4096], P('blk', 'grp'), may hold values from -6 to 6
- picture_projector: bfloat16 [6144, 1024], P('grp'), may hold values from -0.3046875 to 0.3046875
- caption_projector: bfloat16 [4096, 1024], P('grp'), may hold values from -0.375 to 0.375
- score_heat_param: float32 [1], replicated, may hold values from 5 to 15
- score_shift_param: float32 [1], replicated, may hold values from -5 to -2
- objective_cotangent: float32 [1], replicated, may hold values from 16384 to 65536
Outputs:
- image_grad: bfloat16 [8192, 6144], P('blk', 'grp')
- text_grad: bfloat16 [8192, 4096], P('blk', 'grp')
- image_proj_grad: float32 [6144, 1024], P(('grp', 'blk'))
- text_proj_grad: float32 [4096, 1024], P(('grp', 'blk'))
All inputs are finite; a program needn't handle non-finite values.
Results may differ from a plain program's by a relative error of at most 0.02.
Values may be sent and summed in bfloat16 or wider, within the bound.
A program may use at most 128 MiB of HBM per device.

v0:
```python
import jax
import jax.numpy as jnp
from jax import lax
from jax.sharding import PartitionSpec as P


def unit(emb):
    return emb * lax.rsqrt(jnp.sum(emb * emb, axis=-1, keepdims=True) + 1e-06)


def tile_coefficients(
    image_unit_vectors,
    text_block_slice,
    pair_diagonal,
    sharpness_heat,
    logit_offset_value,
    multiplier_amount,
):
    similarity_scores = (
        sharpness_heat
        * jnp.einsum(
            "re,ce->rc", image_unit_vectors, text_block_slice, preferred_element_type=jnp.float32
        )
        + logit_offset_value
    )
    return (multiplier_amount * (jax.nn.sigmoid(similarity_scores) - pair_diagonal)).astype(
        jnp.bfloat16
    )


def per_device(
    picture_tower_mean,
    caption_tower_mean,
    picture_projector,
    caption_projector,
    score_heat_param,
    score_shift_param,
    objective_cotangent,
):
    record_number = picture_tower_mean.shape[0]
    groups = lax.axis_size("grp")
    group_sequence = lax.axis_size("blk")
    share = record_number // groups
    group_idx = lax.axis_index("grp")
    block_idx = lax.axis_index("blk")
    sharpness_heat = score_heat_param[0]
    logit_offset_value = score_shift_param[0]
    multiplier_amount = objective_cotangent[0] * sharpness_heat / (record_number * group_sequence)
    img_part = jnp.dot(picture_tower_mean, picture_projector, preferred_element_type=jnp.float32)
    txt_part = jnp.dot(caption_tower_mean, caption_projector, preferred_element_type=jnp.float32)
    img_emb = lax.psum(img_part, "grp")
    image_unit_vectors = unit(img_emb).astype(jnp.bfloat16)
    txt_share = lax.psum_scatter(txt_part, "grp", scatter_dimension=0, tiled=True)
    text_units = unit(txt_share).astype(jnp.bfloat16)
    row_ids = jnp.arange(record_number)[:, None]
    every_text_row = lax.all_gather(text_units, "blk", axis=0, tiled=True)
    col_ids = jnp.arange(group_sequence * share)[None, :]
    pair_diagonal = (
        (col_ids // share == block_idx) & (row_ids == group_idx * share + col_ids % share)
    ).astype(jnp.float32)
    pair_coefficient = tile_coefficients(
        image_unit_vectors,
        every_text_row,
        pair_diagonal,
        sharpness_heat,
        logit_offset_value,
        multiplier_amount,
    )
    img_unit_part = jnp.dot(pair_coefficient, every_text_row, preferred_element_type=jnp.float32)
    columns = pair_coefficient
    txt_unit_grad = lax.psum_scatter(
        jnp.einsum("rc,re->ce", columns, image_unit_vectors, preferred_element_type=jnp.float32),
        "blk",
        scatter_dimension=0,
        tiled=True,
    )
    _, txt_back = jax.vjp(unit, txt_share)
    txt_grad_share = txt_back(txt_unit_grad)[0].astype(jnp.bfloat16)
    img_unit_grad = lax.psum(img_unit_part.astype(jnp.bfloat16), "grp").astype(jnp.float32)
    _, img_back = jax.vjp(unit, img_emb)
    img_emb_grad = img_back(img_unit_grad)[0].astype(jnp.bfloat16)
    txt_emb_grad = lax.all_gather(txt_grad_share, "grp", axis=0, tiled=True)
    image_grad = jnp.einsum(
        "re,ke->rk", img_emb_grad, picture_projector, preferred_element_type=jnp.float32
    ).astype(jnp.bfloat16)
    text_grad = jnp.einsum(
        "re,ke->rk", txt_emb_grad, caption_projector, preferred_element_type=jnp.float32
    ).astype(jnp.bfloat16)
    columns = picture_tower_mean
    image_proj_grad = lax.psum_scatter(
        jnp.einsum("rk,re->ke", columns, img_emb_grad, preferred_element_type=jnp.float32),
        "blk",
        scatter_dimension=0,
        tiled=True,
    )
    columns = caption_tower_mean
    text_proj_grad = lax.psum_scatter(
        jnp.einsum("rk,re->ke", columns, txt_emb_grad, preferred_element_type=jnp.float32),
        "blk",
        scatter_dimension=0,
        tiled=True,
    )
    return (image_grad, text_grad, image_proj_grad, text_proj_grad)


def solution(mesh):
    placed = (P("blk", "grp"), P("blk", "grp"), P("grp", None), P("grp", None), P(), P(), P())
    return jax.shard_map(
        per_device,
        mesh=mesh,
        in_specs=placed,
        out_specs=(
            P("blk", "grp"),
            P("blk", "grp"),
            P(("grp", "blk"), None),
            P(("grp", "blk"), None),
        ),
        check_vma=False,
    )
```

profile of v0, /device:TPU:2, one launch (start us, length us, event | category | flops | bytes accessed | tf_op | source)
XLA Modules:
  0.0 1419.8 jit_solution(7407624768675881053)
XLA Ops:
  7.2 0.0 copy-start
  7.2 0.0 reduce-scatter.9.cloned.1.call-start
  7.2 3.1 fusion.23
  10.3 0.0 reduce-scatter.9.cloned.1.call-update
  10.3 0.0 all-reduce.3.cloned.1.call-start
  10.4 0.0 copy-done
  10.4 2.4 fusion.22
  12.7 0.0 all-reduce.3.cloned.1.call-update
  12.8 0.0 all-gather.2.cloned.1.call-start
  12.8 33.7 %reduce-scatter.9.cloned.1.call-done = f32[32,1024]{1,0:T(8,128)} async-done(((f32[128,1024]{1,0:T(8,128)}), f32[32,1024]{1,0:T(8,128)}) %reduce-scatter.9.cloned.1.call-update) | async-done | bytes 131088 | tf_op jit(solution)/shard_map/reduce_scatter | solution.py:53
  46.5 1.0 multiply_reduce_fusion.2
  47.6 1.6 multiply_convert_fusion.1
  49.2 0.0 all-gather.2.cloned.1.call-update
  49.2 0.0 all-reduce.5.cloned.1.call-start
  51.2 44.9 %all-reduce.3.cloned.1.call-done = f32[128,1024]{1,0:T(8,128)} async-done(((f32[128,1024]{1,0:T(8,128)}), f32[128,1024]{1,0:T(8,128)}) %all-reduce.3.cloned.1.call-update) | async-done | bytes 524304 | tf_op jit(solution)/shard_map/psum | solution.py:51
  96.1 1.2 multiply_reduce_fusion
  97.3 294.2 %all-gather.2.cloned.1.call-done = bf16[2048,1024]{1,0:T(8,128)(2,1)} async-done(((bf16[32,1024]{1,0:T(8,128)(2,1)}), bf16[2048,1024]{1,0:T(8,128)(2,1)}) %all-gather.2.cloned.1.call-update) | async-done | bytes 4194320 | tf_op jit(solution)/shard_map/all_gather | solution.py:56
  391.5 0.0 copy-start.1
  391.5 4.2 fusion.7
  395.8 0.0 copy-start.2
  395.8 0.9 copy-done.2
  396.6 0.0 copy-done.1
  396.6 1.4 convolution_convert_fusion.2
  398.1 0.0 all-reduce.5.cloned.1.call-update
  398.1 0.0 reduce-scatter.11.cloned.1.call-start
  398.1 5.7 fusion.21
  403.9 0.0 reduce-scatter.11.cloned.1.call-update
  403.9 0.0 reduce-scatter.13.cloned.1.call-start
  404.0 47.7 %all-reduce.5.cloned.1.call-done = bf16[128,1024]{1,0:T(8,128)(2,1)} async-done(((bf16[128,1024]{1,0:T(8,128)(2,1)}), bf16[128,1024]{1,0:T(8,128)(2,1)}) %all-reduce.5.cloned.1.call-update) | async-done | bytes 262160 | tf_op jit(solution)/shard_map/psum | solution.py:79
  451.6 1.2 fusion.9
  452.9 1.3 fusion.10
  454.2 4.6 convolution_bitcast_fusion
  458.7 6.6 copy.15
  465.4 0.0 reduce-scatter.13.cloned.1.call-update
  465.4 0.0 reduce-scatter.15.cloned.1.call-start
  465.4 304.7 %reduce-scatter.11.cloned.1.call-done = f32[32,1024]{1,0:T(8,128)} async-done(((f32[2048,1024]{1,0:T(8,128)}), f32[32,1024]{1,0:T(8,128)}) %reduce-scatter.11.cloned.1.call-update) | async-done | bytes 131088 | tf_op jit(solution)/shard_map/reduce_scatter | solution.py:71
  770.1 0.0 copy-done.4
  770.1 1.0 multiply_reduce_fusion.1
  771.2 1.0 fusion.11
  772.2 7.3 all_gather.7
  779.5 0.7 copy-done.3
  780.2 3.6 convolution_bitcast_fusion.1
  783.8 5.3 copy.17
  789.2 0.0 reduce-scatter.15.cloned.1.call-update
  789.2 1.9 convolution_convert_fusion
  791.1 3.2 convolution_convert_fusion.1
  794.4 300.0 %reduce-scatter.13.cloned.1.call-done = f32[24,1024]{1,0:T(8,128)} async-done(((f32[1536,1024]{1,0:T(8,128)}), f32[24,1024]{1,0:T(8,128)}) %reduce-scatter.13.cloned.1.call-update) | async-done | bytes 98320
  1094.4 318.5 %reduce-scatter.15.cloned.1.call-done = f32[16,1024]{1,0:T(8,128)} async-done(((f32[1024,1024]{1,0:T(8,128)}), f32[16,1024]{1,0:T(8,128)}) %reduce-scatter.15.cloned.1.call-update) | async-done | bytes 65552
  (8 shorter events, 0.1 us)
Async XLA Ops:
  7.2 3.2 copy-start
  7.2 39.4 %reduce-scatter.9.cloned.1.call-start = ((), (), s32[]{:S(2)}) async-start(), calls=%async_computation.5 | async-start | bytes 655360 | tf_op jit(solution)/shard_map/reduce_scatter | solution.py:53
  10.3 85.8 %all-reduce.3.cloned.1.call-start = ((), (), s32[]{:S(2)}) async-start(), calls=%async_computation.4 | async-start | bytes 1048576 | tf_op jit(solution)/shard_map/psum | solution.py:51
  12.8 378.8 %all-gather.2.cloned.1.call-start = ((), (), s32[]{:S(2)}) async-start(), calls=%async_computation.6 | async-start | bytes 4259840 | tf_op jit(solution)/shard_map/all_gather | solution.py:56
  49.2 402.4 %all-reduce.5.cloned.1.call-start = ((), (), s32[]{:S(2)}) async-start(), calls=%async_computation.7 | async-start | bytes 524288 | tf_op jit(solution)/shard_map/psum | solution.py:79
  391.5 5.1 copy-start.1
  395.8 0.9 copy-start.2
  398.1 372.0 %reduce-scatter.11.cloned.1.call-start = ((), (), s32[]{:S(2)}) async-start(), calls=%async_computation.8 | async-start | bytes 8519680 | tf_op jit(solution)/shard_map/reduce_scatter | solution.py:71
  403.9 690.5 %reduce-scatter.13.cloned.1.call-start = ((), (), s32[]{:S(2)}) async-start(), calls=%async_computation.9 | async-start | bytes 6389760
  465.4 304.8 %copy-start.4 = (f32[32,1024]{1,0:T(8,128)S(1)}, f32[32,1024]{1,0:T(8,128)}, u32[]{:S(2)}) copy-start(f32[32,1024]{1,0:T(8,128)} %reduce-scatter.9.cloned.1.call-done) | copy-start | bytes 393220
  465.4 947.5 %reduce-scatter.15.cloned.1.call-start = ((), (), s32[]{:S(2)}) async-start(), calls=%async_computation.10 | async-start | bytes 4259840
  779.5 0.7 copy-start.3
Sparse Core Ops, SparseCore 0:
  10.8 35.7 reduce-scatter.8
  49.4 46.6 all-reduce.2
  98.6 292.8 all-gather.1
  398.2 53.3 all-reduce.4
  454.0 316.0 reduce-scatter.10
  773.1 321.2 reduce-scatter.12
  1097.6 315.2 reduce-scatter.14
where the time goes:
time: 1440 us; the launch traced here: 1420 us
  waiting for transfers between devices  1340 us (93%)
  matrix products  30.2 us (2%)
  between operations  16.1 us (1%)
    unnamed x9, waiting for transfers between devices  619 us
    reduce_scatter x1, waiting for transfers between devices, per_device(): lax.psum_scatter(jnp.einsum('rc,re->ce', columns, image_unit_vectors, pre...  305 us
    all_gather x1, waiting for transfers between devices, per_device(): every_text_row = lax.all_gather(text_units, 'blk', axis=0, tiled=True)  294 us
    psum x1, waiting for transfers between devices, per_device(): lax.psum(img_unit_part.astype(jnp.bfloat16), 'grp').astype(jnp.float32)  47.7 us
    psum x1, waiting for transfers between devices, per_device(): img_emb = lax.psum(img_part, 'grp')  44.9 us
    reduce_scatter x1, waiting for transfers between devices, per_device(): lax.psum_scatter(txt_part, 'grp', scatter_dimension=0, tiled=True)  33.7 us
  transfers between devices with their start and end apart: 7, of which 7 were waited for; matrix products, arithmetic and copies ran while one was open for 3% of the time, Pallas kernels for 0%

commit v1 on v0

v1 whole, which is shorter than its diff:
```python
import functools

import jax
import jax.numpy as jnp
from jax import lax
from jax.experimental import pallas as pl
from jax.experimental.pallas import tpu as pltpu
from jax.sharding import PartitionSpec as P

MESH = pl.DeviceIdType.MESH
F32 = jnp.float32
BF16 = jnp.bfloat16
EPS = 1e-06

ROWS = 128
SHARE = 32
HALF = 16
EMB = 1024
WIDE = 512
FI, FT = 1536, 1024
FIY, FTY = FI // 4, FT // 4
OI, OT = FIY // 16, FTY // 16
CHUNK = 512
SENDS = 112


def dot_nn(a, b):
    return lax.dot_general(a, b, (((1,), (0,)), ((), ())), preferred_element_type=F32)


def dot_nt(a, b):
    return lax.dot_general(a, b, (((1,), (1,)), ((), ())), preferred_element_type=F32)


def dot_tn(a, b):
    return lax.dot_general(a, b, (((0,), (0,)), ((), ())), preferred_element_type=F32)


def scratch():
    v = pltpu.VMEM
    dma = pltpu.SemaphoreType.DMA
    return dict(
        xi=v((ROWS, FI), BF16),
        xt=v((ROWS, FT), BF16),
        wi=v((FI, EMB), BF16),
        wt=v((FT, EMB), BF16),
        part=v((2, ROWS, EMB), F32),
        a_out=v((2, 2, SHARE, EMB), BF16),
        a_in=v((2, 2, SHARE, EMB), BF16),
        half=v((2, SHARE, EMB), F32),
        b_out=v((2, SHARE, EMB), BF16),
        b_in=v((2, SHARE, EMB), BF16),
        emb=v((2, SHARE, EMB), F32),
        rst=v((2, SHARE, 128), F32),
        iu=v((2, 4, 4, SHARE, WIDE), BF16),
        tu=v((2, 8, SHARE, EMB), BF16),
        coef=v((2, 512, 256), BF16),
        c_out=v((8, SHARE, EMB), BF16),
        c_in=v((8, SHARE, EMB), BF16),
        own_t=v((8, SHARE, EMB), F32),
        d_out=v((4, 2, SHARE, EMB), BF16),
        d_in=v((4, 2, SHARE, EMB), BF16),
        own_i=v((2, 4, 4, SHARE, WIDE), F32),
        e1_out=v((2, 4, 4, SHARE, WIDE), BF16),
        e1_in=v((2, 4, 4, SHARE, WIDE), BF16),
        mid_i=v((2, 4, SHARE, WIDE), F32),
        e2_out=v((2, 4, SHARE, WIDE), BF16),
        e2_in=v((2, 4, SHARE, WIDE), BF16),
        sum_i=v((SHARE, EMB), F32),
        gi=v((2, 4, 2, SHARE, EMB), BF16),
        gt=v((2, 4, 2, SHARE, EMB), BF16),
        ti=v((4, ROWS, FIY), BF16),
        tt=v((4, ROWS, FTY), BF16),
        mi=v((512, FIY), BF16),
        mt=v((512, FTY), BF16),
        ni=v((2, FIY, 256), BF16),
        nt=v((2, FTY, 256), BF16),
        pi=v((FIY, EMB), F32),
        pt=v((FTY, EMB), F32),
        fi_out=v((2, 4, 2, 2 * OI, WIDE), BF16),
        fi_in=v((2, 3, 2, 2 * OI, WIDE), BF16),
        fi_end=v((2, 2, 2 * OI, WIDE), BF16),
        fi_side=v((2, 2 * OI, WIDE), BF16),
        ft_out=v((2, 4, 2, OT, EMB), BF16),
        ft_in=v((2, 3, 2, OT, EMB), BF16),
        ft_end=v((2, 2, OT, EMB), BF16),
        ft_side=v((2, OT, EMB), BF16),
        in_sem=dma((7,)),
        x_sem=dma((2, 4)),
        a_sem=dma((2,)),
        b_sem=dma((2,)),
        iu_sem=dma((2, 2, 4)),
        tu_sem=dma((9,)),
        tc_sem=dma((2,)),
        c_sem=dma((2,)),
        d_sem=dma((4, 2)),
        e1_sem=dma((2, 4)),
        e2_sem=dma((2, 4)),
        far_sem=dma((2,)),
        g_sem=dma((2, 2, 4)),
        gc_sem=dma((2, 3)),
        f_sem=dma((2, 2, 3)),
        end_sem=dma((2, 2, 2)),
        h_sem=dma((2,)),
        send_sem=dma((SENDS,)),
    )


NAMES = tuple(scratch())
AROUND = (0, 1, -1, 2, -2, 3, -3, 4)
ABOUT = (0, 1, -1, 2)


def rows_half(h):
    return pl.ds(h * HALF, HALF)


def interleave(order, **tasks):
    for name in order:
        next(tasks[name], None)
    left = list(tasks.values())
    while left:
        left = [task for task in left if next(task, True) is not True]


def together(*tasks):
    left = list(tasks)
    while left:
        left = [task for task in left if next(task, True) is not True]
        if left:
            yield


def kernel(xi_h, xt_h, wi_h, wt_h, heat_ref, shift_ref, cot_ref, og_i, og_t, op_i, op_t, *refs):
    s = dict(zip(NAMES, refs))
    g = lax.axis_index("grp")
    b = lax.axis_index("blk")
    xh, co = lax.div(g, 2), lax.rem(g, 2)
    y, xl, z = lax.div(b, 16), lax.rem(lax.div(b, 8), 2), lax.rem(b, 8)
    x = xh * 2 + xl
    oc, ox = 1 - co, 1 - xh

    def dev(x_, y_, z_, co_):
        return (lax.div(x_, 2) * 2 + co_, (y_ * 2 + lax.rem(x_, 2)) * 8 + z_)

    other_core = dev(x, y, z, oc)
    near = dev(xh * 2 + (1 - xl), y, z, co)
    along_x = {k: dev(lax.rem(x + 4 + k, 4), y, z, co) for k in (1, -1, 2)}
    far = along_x[2]
    along_y = {k: dev(x, lax.rem(y + 4 + k, 4), z, co) for k in (1, -1, 2)}
    along_z = {k: dev(x, y, lax.rem(z + 8 + k, 8), co) for k in (1, -1, 2, -2)}
    corner = {
        (h, k): dev(xh * 2 + h, y, lax.rem(z + 8 + k, 8), co) for h in range(2) for k in (1, -1)
    }
    corners = [dev(xh * 2 + (1 - xl), y, lax.rem(z + 8 + k, 8), co) for k in (1, -1)]

    sends = []

    def send(src, dst, sem, to):
        copy = pltpu.make_async_remote_copy(
            src_ref=src,
            dst_ref=dst,
            send_sem=s["send_sem"].at[len(sends)],
            recv_sem=sem,
            device_id=to,
            device_id_type=MESH,
        )
        copy.start()
        sends.append(copy)

    def arrived(dst, sem):
        pltpu.make_async_copy(dst, dst, sem).wait()

    def gather_eight(to, ref, sem, then):
        for way in (2, -2, 1, -1):
            send(ref(0, None), ref(-way, None), sem(-way), to[way])
        yield
        for half, way in enumerate((1, -1)):
            far_ = -2 * way
            arrived(ref(far_, None), sem(far_))
            send(ref(far_, half), ref(4, half), s["tu_sem"].at[7 + half], to[2 * way])
            send(ref(far_, None), ref(-3 * way, None), sem(-3 * way), to[way])
        for k in (1, -1):
            arrived(ref(k, None), sem(k))
        then(0)
        yield
        for k in (3, -3):
            arrived(ref(k, None), sem(k))
        for half in range(2):
            arrived(ref(4, half), s["tu_sem"].at[7 + half])
        then(1)

    def scatter_eight(to, own, out, inn, sem, totals):
        for n, way in enumerate((1, -1)):
            rows = rows_half(n)
            out[3, n, rows] = own(4)[n * HALF : (n + 1) * HALF].astype(BF16)
            send(out.at[3, n, rows], inn.at[3, n, rows], sem.at[3, n], to[2 * way])
        for n, way in enumerate((1, -1)):
            out[2, n] = own(3 * way).astype(BF16)
            send(out.at[2, n], inn.at[2, n], sem.at[2, n], to[way])
        for n, way in enumerate((1, -1)):
            out[0, n] = own(way).astype(BF16)
            send(out.at[0, n], inn.at[0, n], sem.at[0, n], to[way])
        yield
        for n, way in enumerate((1, -1)):
            rows = slice(n * HALF, (n + 1) * HALF)
            rest = slice((1 - n) * HALF, (2 - n) * HALF)
            value = own(2 * way)
            arrived(inn.at[2, n], sem.at[2, n])
            arrived(inn.at[3, n, rows_half(n)], sem.at[3, n])
            more = inn[2, n, rows].astype(F32) + inn[3, n, rows].astype(F32)
            out[1, n, rows] = (value[rows] + more).astype(BF16)
            out[1, n, rest] = (value[rest] + inn[2, n, rest].astype(F32)).astype(BF16)
            send(out.at[1, n], inn.at[1, n], sem.at[1, n], to[2 * way])
        value = own(0)
        yield
        for m in range(2):
            for n in range(2):
                arrived(inn.at[m, n], sem.at[m, n])
                value = value + inn[m, n].astype(F32)
        totals.append(value)

    def gather_four(to, ref, sem):
        for way in (1, -1):
            send(ref(0, None), ref(-way, None), sem.at[0 if way > 0 else 1], to[way])
        yield
        for way in (1, -1):
            n = 0 if way > 0 else 1
            arrived(ref(-way, None), sem.at[n])
            send(ref(-way, n), ref(2, n), sem.at[2 + n], to[way])
        yield
        for n in range(2):
            arrived(ref(2, n), sem.at[2 + n])

    def gather_direct(to, ref, sem):
        for way in (2, 1, -1):
            send(ref(0, None), ref(-way, None), sem.at[-way % 4], to[way])
        yield
        for k in (1, -1, 2):
            arrived(ref(k, None), sem.at[k % 4])

    def scatter_direct(to, own, out, inn, sem, totals):
        for way in (2, 1, -1):
            k = -way % 4
            out[k] = own(way).astype(BF16)
            send(out.at[k], inn.at[k], sem.at[k], to[way])
        value = own(0)
        yield
        for k in (1, -1, 2):
            arrived(inn.at[k % 4], sem.at[k % 4])
            value = value + inn[k % 4].astype(F32)
        totals.append(value)

    def scatter_corner(t, own, name, totals):
        out, inn, end, side = (s[name + part] for part in ("_out", "_in", "_end", "_side"))
        sem, end_sem = s["f_sem"].at[t], s["end_sem"].at[t]
        for step in range(1, 5):
            if step > 1:
                yield
            for d, way in enumerate((1, -1)):
                if step == 1:
                    out[d, 0, d] = own(4 * way, d).astype(BF16)
                    send(out.at[d, 0, d], inn.at[d, 0, d], sem.at[d, 0], along_z[way])
                    continue
                before = inn.at[d, step - 2]
                arrived(before.at[d] if step == 2 else before, sem.at[d, step - 2])
                for half in range(2):
                    value = own(way * (5 - step), half)
                    if step > 2 or half == d:
                        value = value + inn[d, step - 2, half].astype(F32)
                    out[d, step - 1, half] = value.astype(BF16)
                    if step == 4:
                        origin = lax.rem(xl + half, 2)
                        send(out.at[d, 3, half], end.at[origin, d], end_sem.at[origin, d], corner[half, way])
                if step < 4:
                    send(out.at[d, step - 1], inn.at[d, step - 1], sem.at[d, step - 1], along_z[way])
            if step == 1:
                side[0] = own(0, 1 - xl).astype(BF16)
                send(side.at[0], side.at[1], s["h_sem"].at[t], near)
        value = own(0, xl)
        yield
        arrived(side.at[1], s["h_sem"].at[t])
        value = value + side[1].astype(F32)
        for origin in range(2):
            for d in range(2):
                arrived(end.at[origin, d], end_sem.at[origin, d])
                value = value + end[origin, d].astype(F32)
        totals.append(value)

    def load(src, dst, n):
        copy = pltpu.make_async_copy(src, dst, s["in_sem"].at[n])
        copy.start()
        return copy

    def load_rows(src, dst, k, n):
        rows = pl.ds(k * CHUNK, CHUNK)
        return load(src.at[rows], dst.at[rows], n)

    xi_load = load(xi_h, s["xi"], 0)
    wi_loads = [load_rows(wi_h, s["wi"], k, 1 + k) for k in range(FI // CHUNK)]
    xt_load = load(xt_h, s["xt"], 4)
    wt_loads = [load_rows(wt_h, s["wt"], k, 5 + k) for k in range(FT // CHUNK)]

    barrier = pltpu.get_barrier_semaphore()
    peers = [other_core, *along_x.values(), *along_y.values(), *along_z.values(), *corners]
    for to in peers:
        pl.semaphore_signal(barrier, inc=1, device_id=to, device_id_type=MESH)

    def partial(t, x_ref, w_ref, x_load, w_loads):
        x_load.wait()
        for k, w_load in enumerate(w_loads):
            w_load.wait()
            rows = slice(k * CHUNK, (k + 1) * CHUNK)
            part = dot_nn(x_ref[:, rows], w_ref[rows, :])
            s["part"][t] = part if k == 0 else s["part"][t] + part
            yield
        for h in range(2):
            rows = pl.ds(pl.multiple_of((h * 2 + oc) * SHARE, SHARE), SHARE)
            s["a_out"][t, h] = s["part"][t, rows, :].astype(BF16)
        send(s["a_out"].at[t], s["a_in"].at[t], s["a_sem"].at[t], other_core)

    def mine(t, h):
        rows = pl.ds(pl.multiple_of((h * 2 + co) * SHARE, SHARE), SHARE)
        got = s["a_in"][t, pl.ds(h, 1)].reshape(SHARE, EMB)
        return s["part"][t, rows, :] + got.astype(F32)

    def to_far(t):
        arrived(s["a_in"].at[t], s["a_sem"].at[t])
        s["b_out"][t] = mine(t, ox).astype(BF16)
        send(s["b_out"].at[t], s["b_in"].at[t], s["b_sem"].at[t], far)
        s["half"][t] = mine(t, xh)

    def exchange(t, x_ref, t_ref, width):
        for k, to in along_y.items():
            cols = pl.ds(pl.multiple_of(lax.rem(y + 4 + k, 4) * width, 128), width)
            send(x_ref.at[:, cols], t_ref.at[-k % 4], s["x_sem"].at[t, -k % 4], to)
        cols = pl.ds(pl.multiple_of(y * width, 128), width)
        t_ref[0] = x_ref[:, cols]

    image_part = partial(0, s["xi"], s["wi"], xi_load, wi_loads)
    text_part = partial(1, s["xt"], s["wt"], xt_load, wt_loads)
    for _ in wi_loads:
        next(image_part)
    pl.semaphore_wait(barrier, len(peers))
    next(image_part, None)
    for _ in text_part:
        pass
    to_far(0)
    exchange(0, s["xi"], s["ti"], FIY)
    to_far(1)
    exchange(1, s["xt"], s["tt"], FTY)

    def units(t):
        arrived(s["b_in"].at[t], s["b_sem"].at[t])
        e = s["half"][t] + s["b_in"][t].astype(F32)
        rs = lax.rsqrt(jnp.sum(e * e, axis=-1, keepdims=True) + EPS)
        s["emb"][t] = e
        s["rst"][t] = jnp.broadcast_to(rs, (SHARE, 128))
        return (e * rs).astype(BF16)

    def images_ring(w):
        def one(k, half):
            at = (k % 4, 0) if w == 0 else (0, k % 4)
            rows = pl.ds(0, SHARE) if half is None else rows_half(half)
            return s["iu"].at[(w,) + at + (rows,)]

        def four(k, half):
            rows = pl.ds(0, SHARE) if half is None else rows_half(half)
            at = (pl.ds(0, 4), k % 4) if w == 0 else (k % 4, pl.ds(0, 4))
            return s["iu"].at[(w,) + at + (rows,)]

        first, second = (along_x, along_y) if w == 0 else (along_y, along_x)
        yield from gather_direct(first, one, s["iu_sem"].at[w, 0])
        yield from gather_direct(second, four, s["iu_sem"].at[w, 1])

    def texts_ring():
        s["tu"][0, 0] = units(1)

        def ref(k, half):
            rows = pl.ds(0, SHARE) if half is None else rows_half(half)
            return s["tu"].at[0, AROUND.index(k), rows]

        def sem(k):
            return s["tu_sem"].at[AROUND.index(k)]

        def across(part):
            slots = (pl.ds(0, 5), pl.ds(5, 3))[part]
            send(s["tu"].at[0, slots], s["tu"].at[1, slots], s["tc_sem"].at[part], other_core)

        yield from gather_eight(along_z, ref, sem, across)

    def images_rings():
        u = units(0)
        for w in range(2):
            s["iu"][w, 0, 0] = u[:, w * WIDE : (w + 1) * WIDE]
        yield from together(images_ring(0), images_ring(1))

    def turned(t, t_ref, m_ref, n_ref):
        for k in range(1, 4):
            arrived(t_ref.at[k], s["x_sem"].at[t, k])
        for n, core in enumerate((co, oc)):
            for k, dy in enumerate(ABOUT):
                for h in range(2):
                    at = (n * 8 + k * 2 + h) * SHARE
                    rows = pl.ds(pl.multiple_of((h * 2 + core) * SHARE, SHARE), SHARE)
                    m_ref[at : at + SHARE, :] = t_ref[dy % 4, rows, :]
            n_ref[n] = m_ref[n * 256 : (n + 1) * 256, :].T
            yield

    def towers():
        yield from turned(0, s["ti"], s["mi"], s["ni"])
        yield from turned(1, s["tt"], s["mt"], s["nt"])

    interleave("ititti", t=texts_ring(), i=images_rings())

    heat, shift = heat_ref[0], shift_ref[0]
    mult = cot_ref[0] * heat / 8192.0

    def texts(n, w):
        return s["tu"][n].reshape(256, EMB)[:, w * WIDE : (w + 1) * WIDE]

    def images(w):
        return s["iu"][w].reshape(512, WIDE)

    def coefficients(n):
        score = dot_nt(images(0), texts(n, 0)) + dot_nt(images(1), texts(n, 1))
        value = jax.nn.sigmoid(heat * score + shift)
        if n == 0:
            row = lax.broadcasted_iota(jnp.int32, (512, 256), 0)
            col = lax.broadcasted_iota(jnp.int32, (512, 256), 1)
            value = value - ((row == col) & (row < SHARE)).astype(F32)
        s["coef"][n] = (mult * value).astype(BF16)

    def text_half(n, w, out):
        grad = dot_tn(s["coef"][n], images(w)).reshape(8, SHARE, WIDE)
        out[:, :, w * WIDE : (w + 1) * WIDE] = grad.astype(out.dtype)

    coefficients(0)
    arrived(s["tu"].at[1, pl.ds(0, 5)], s["tc_sem"].at[0])
    arrived(s["tu"].at[1, pl.ds(5, 3)], s["tc_sem"].at[1])
    coefficients(1)
    for w in range(2):
        text_half(1, w, s["c_out"])
        cols = pl.ds(w * WIDE, WIDE)
        send(s["c_out"].at[:, :, cols], s["c_in"].at[:, :, cols], s["c_sem"].at[w], other_core)

    def back(t, grads, grad):
        rs = s["rst"][t][:, :1]
        u = s["emb"][t] * rs
        value = (grad - u * jnp.sum(u * grad, axis=-1, keepdims=True)) * rs
        grads[0, 0, pl.ds(xh, 1)] = value.astype(BF16).reshape(1, SHARE, EMB)

    def text_grad():
        for w in range(2):
            text_half(0, w, s["own_t"])
        for w in range(2):
            cols = pl.ds(w * WIDE, WIDE)
            arrived(s["c_in"].at[:, :, cols], s["c_sem"].at[w])

        def own(k):
            at = AROUND.index(k)
            return s["own_t"][at] + s["c_in"][at].astype(F32)

        totals = []
        yield from scatter_eight(along_z, own, s["d_out"], s["d_in"], s["d_sem"], totals)
        back(1, s["gt"], totals[0])

    def image_half(w):
        grad = dot_nn(s["coef"][0], texts(0, w)) + dot_nn(s["coef"][1], texts(1, w))
        s["own_i"][w] = grad.reshape(4, 4, SHARE, WIDE)

        def four(k):
            return s["own_i"][0, :, k % 4] if w == 0 else s["own_i"][1, k % 4]

        def one(k):
            return s["mid_i"][w, k % 4]

        first, second = (along_y, along_x) if w == 0 else (along_x, along_y)
        totals = []
        yield from scatter_direct(
            first, four, s["e1_out"].at[w], s["e1_in"].at[w], s["e1_sem"].at[w], totals
        )
        s["mid_i"][w] = totals[0]
        totals = []
        yield from scatter_direct(
            second, one, s["e2_out"].at[w], s["e2_in"].at[w], s["e2_sem"].at[w], totals
        )
        s["sum_i"][:, w * WIDE : (w + 1) * WIDE] = totals[0]

    def image_grad():
        yield from together(image_half(0), image_half(1))
        back(0, s["gi"], s["sum_i"][...])

    def spread(t, grads, first_dot):
        def across(slots, h, n):
            send(grads.at[0, slots, h], grads.at[1, slots, h], s["gc_sem"].at[t, n], other_core)

        def ring(h, n):
            def ref(k, half):
                rows = pl.ds(0, SHARE) if half is None else rows_half(half)
                return grads.at[0, ABOUT.index(k if k != -2 else 2), h, rows]

            if n == 0:
                send(ref(0, None), ref(0, None), s["far_sem"].at[t], far)
            else:
                arrived(ref(0, None), s["far_sem"].at[t])
            task = gather_four(along_y, ref, s["g_sem"].at[t, n])
            next(task)
            yield
            next(task)
            if n == 1:
                across(pl.ds(0, 3), h, 1)
            yield
            yield from task
            across(pl.ds(0, 4) if n == 0 else pl.ds(3, 1), h, 2 * n)

        first, second = ring(xh, 0), ring(ox, 1)
        next(first)
        yield
        next(first)
        next(second)
        yield
        next(first, None)
        next(second)
        yield
        next(second, None)
        first_dot()
        yield
        for n, (h, slots) in enumerate(((xh, pl.ds(0, 4)), (ox, pl.ds(0, 3)), (ox, pl.ds(3, 1)))):
            arrived(grads.at[1, slots, h], s["gc_sem"].at[t, n])

    def weights(t, grads, n_ref, p_ref, own, names, w_ref, out):
        def term(n):
            return dot_nn(n_ref[n], grads[n].reshape(256, EMB))

        def first_dot():
            p_ref[...] = term(0)

        yield from spread(t, grads, first_dot)
        p_ref[...] = p_ref[...] + term(1)
        totals = []
        ring = scatter_corner(t, own, names, totals)
        chunks = [slice(k, k + CHUNK) for k in range(0, w_ref.shape[0], CHUNK)]
        for _ in ring:
            for cols in (chunks.pop(0),) if chunks else ():
                value = dot_nt(grads[:, 0].reshape(ROWS, EMB), w_ref[cols, :]).astype(BF16)
                for n, core in enumerate((co, oc)):
                    for h in range(2):
                        rows = pl.ds(pl.multiple_of((h * 2 + core) * SHARE, SHARE), SHARE)
                        at = (n * 2 + h) * SHARE
                        out[rows, cols] = value[at : at + SHARE]
            yield
        return totals[0]

    def own_i(k, half):
        n = half * 8 + lax.rem(z + 8 + k, 8)
        rows = s["pi"][pl.ds(pl.multiple_of(n * OI, 8), OI), :]
        return jnp.concatenate([rows[:, :WIDE], rows[:, WIDE:]], axis=0)

    def own_t(k, half):
        n = half * 8 + lax.rem(z + 8 + k, 8)
        return s["pt"][pl.ds(pl.multiple_of(n * OT, 8), OT), :]

    def texts_back():
        yield from text_grad()
        op_t[...] = yield from weights(1, s["gt"], s["nt"], s["pt"], own_t, "ft", s["wt"], og_t)

    def images_back():
        yield from image_grad()
        total = yield from weights(0, s["gi"], s["ni"], s["pi"], own_i, "fi", s["wi"], og_i)
        op_i[:, :WIDE] = total[:OI]
        op_i[:, WIDE:] = total[OI:]

    interleave("itwwtwititwitiititwitititit", i=images_back(), t=texts_back(), w=towers())
    for copy in sends:
        copy.wait_send()


def per_device(xi, xt, wi, wt, heat, shift, cot):
    vmem = pl.BlockSpec(memory_space=pltpu.VMEM)
    smem = pl.BlockSpec(memory_space=pltpu.SMEM)
    hbm = pl.BlockSpec(memory_space=pl.ANY)
    shapes = (
        jax.ShapeDtypeStruct((ROWS, FI), BF16),
        jax.ShapeDtypeStruct((ROWS, FT), BF16),
        jax.ShapeDtypeStruct((OI, EMB), F32),
        jax.ShapeDtypeStruct((OT, EMB), F32),
    )
    return pl.pallas_call(
        kernel,
        out_shape=shapes,
        in_specs=[hbm] * 4 + [smem] * 3,
        out_specs=[vmem] * 4,
        scratch_shapes=list(scratch().values()),
        compiler_params=pltpu.CompilerParams(
            collective_id=0, has_side_effects=True, vmem_limit_bytes=52 * 1024 * 1024
        ),
    )(xi, xt, wi, wt, heat, shift, cot)


def solution(mesh):
    placed = (P("blk", "grp"), P("blk", "grp"), P("grp", None), P("grp", None), P(), P(), P())
    return jax.shard_map(
        per_device,
        mesh=mesh,
        in_specs=placed,
        out_specs=(
            P("blk", "grp"),
            P("blk", "grp"),
            P(("grp", "blk"), None),
            P(("grp", "blk"), None),
        ),
        check_vma=False,
    )
```

time: 1440 us -> 85 us (0.06); the launches traced: 1420 us -> 84.5 us
  waiting for transfers between devices: 1340 us -> 0 us
  Pallas kernels: 0 us -> 77.2 us
  matrix products: 30.2 us -> 0 us
    unnamed x9 -> x0, waiting for transfers between devices: 619 us -> none
    reduce_scatter x2 -> x0, waiting for transfers between devices: 338 us -> none  [the longest x1 305 us: per_device(): lax.psum_scatter(jnp.einsum('rc,re->ce', columns, image_unit_vectors, pre...]
    all_gather x1 -> x0, waiting for transfers between devices: 294 us -> none  [per_device(): every_text_row = lax.all_gather(text_units, 'blk', axis=0, tiled=True)]
    psum x2 -> x0, waiting for transfers between devices: 92.5 us -> none  [the longest x1 47.7 us: per_device(): lax.psum(img_unit_part.astype(jnp.bfloat16), 'grp').astype(jnp.float32)]
    pallas_call x0 -> x1, Pallas kernels: none -> 77.2 us  [per_device(): pl.pallas_call(kernel, out_shape=shapes, in_specs=[hbm] * 4 + [smem] * 3,...]
    dot_general x9 -> x0, matrix products: 30.2 us -> none  [the longest x1 5.73 us: per_device(): jnp.einsum('rc,re->ce', columns, image_unit_vectors, preferred_element_ty...]
  transfers between devices with their start and end apart: 7 -> 0, of which waited for: 7 -> 0; matrix products, arithmetic and copies ran while one was open for 3% -> 0% of each run, Pallas kernels for 0% -> 0%
where the time goes in v1:
time: 85 us; the launch traced here: 84.5 us
  Pallas kernels  77.2 us (91%)
  local copies, waits for them, and re-layouts  4.66 us (5%)
  between operations  2.59 us (3%)
    pallas_call x1, Pallas kernels, per_device(): pl.pallas_call(kernel, out_shape=shapes, in_specs=[hbm] * 4 + [smem] * 3,...  77.2 us
    unnamed x8, local copies, waits for them, and re-layouts  4.66 us

profile of v1, /device:TPU:2, one launch (start us, length us, event | category | flops | bytes accessed | tf_op | source)
XLA Modules:
  0.0 84.5 jit_solution(14566927869644383807)
XLA Ops:
  2.6 0.0 copy-start
  2.6 1.0 %copy-done = bf16[128,1536]{1,0:T(8,128)(2,1)S(1)} copy-done((bf16[128,1536]{1,0:T(8,128)(2,1)S(1)}, bf16[128,1536]{1,0:T(8,128)(2,1)}, u32[]{:S(2)}) %copy-start) | copy-done | bytes 393240
  3.6 0.0 copy-start.1
  3.6 0.9 %copy-done.1 = bf16[128,1024]{1,0:T(8,128)(2,1)S(1)} copy-done((bf16[128,1024]{1,0:T(8,128)(2,1)S(1)}, bf16[128,1024]{1,0:T(8,128)(2,1)}, u32[]{:S(2)}) %copy-start.1) | copy-done | bytes 262168
  4.5 77.2 %shard_map.102 = (bf16[128,1536]{1,0:T(8,128)(2,1)S(1)}, bf16[128,1024]{1,0:T(8,128)(2,1)S(1)}, f32[24,1024]{1,0:T(8,128)S(1)}, f32[16,1024]{1,0:T(8,128)S(1)}) custom-call(bf16[128,1536]{1,0:T(8,128)(2,1)S(1)} %copy-done, bf16[128,1024]{1,0:T(8,128)(2,1)S(1)} %copy-done.1, bf16[1536,1024]{1,0:T(8,128)(2,1)} %wi_h.1, bf16[1024,1024]{1,0:T(8,128)(2,1)} %wt_h.1, ...), custom_call_target="tpu_custom_call" | custom-call | tf_op jit(solution)/shard_map/pallas_call | solution.py:589
  81.7 0.7 copy.18
  82.5 0.7 copy.19
  83.2 0.6 copy.20
  83.8 0.6 copy.21
Async XLA Ops:
  2.6 1.0 %copy-start = (bf16[128,1536]{1,0:T(8,128)(2,1)S(1)}, bf16[128,1536]{1,0:T(8,128)(2,1)}, u32[]{:S(2)}) copy-start(bf16[128,1536]{1,0:T(8,128)(2,1)} %xi_h.1) | copy-start | bytes 1179652
  3.6 0.9 %copy-start.1 = (bf16[128,1024]{1,0:T(8,128)(2,1)S(1)}, bf16[128,1024]{1,0:T(8,128)(2,1)}, u32[]{:S(2)}) copy-start(bf16[128,1024]{1,0:T(8,128)(2,1)} %xt_h.1) | copy-start | bytes 786436

commit v2 on v1

--- a/solution.py
+++ b/solution.py
@@ -52,9 +52,9 @@
         b_in=v((2, SHARE, EMB), BF16),
         emb=v((2, SHARE, EMB), F32),
         rst=v((2, SHARE, 128), F32),
-        iu=v((2, 4, 4, SHARE, WIDE), BF16),
+        iu=v((4, 4, SHARE, EMB), BF16),
         tu=v((2, 8, SHARE, EMB), BF16),
-        coef=v((2, 512, 256), BF16),
+        coef=v((512, 512), BF16),
         c_out=v((8, SHARE, EMB), BF16),
         c_in=v((8, SHARE, EMB), BF16),
         own_t=v((8, SHARE, EMB), F32),
@@ -92,7 +92,7 @@
         iu_sem=dma((2, 2, 4)),
         tu_sem=dma((9,)),
         tc_sem=dma((2,)),
-        c_sem=dma((2,)),
+        c_sem=dma,
         d_sem=dma((4, 2)),
         e1_sem=dma((2, 4)),
         e2_sem=dma((2, 4)),
@@ -123,14 +123,6 @@
         left = [task for task in left if next(task, True) is not True]
 
 
-def together(*tasks):
-    left = list(tasks)
-    while left:
-        left = [task for task in left if next(task, True) is not True]
-        if left:
-            yield
-
-
 def kernel(xi_h, xt_h, wi_h, wt_h, heat_ref, shift_ref, cot_ref, og_i, og_t, op_i, op_t, *refs):
     s = dict(zip(NAMES, refs))
     g = lax.axis_index("grp")
@@ -154,7 +146,7 @@
     }
     corners = [dev(xh * 2 + (1 - xl), y, lax.rem(z + 8 + k, 8), co) for k in (1, -1)]
 
-    sends = []
+    sends, drained = [], []
 
     def send(src, dst, sem, to):
         copy = pltpu.make_async_remote_copy(
@@ -359,15 +351,17 @@
         return (e * rs).astype(BF16)
 
     def images_ring(w):
+        if w == 0:
+            s["iu"][0, 0] = units(0)
+        cols = pl.ds(w * WIDE, WIDE)
+
         def one(k, half):
             at = (k % 4, 0) if w == 0 else (0, k % 4)
-            rows = pl.ds(0, SHARE) if half is None else rows_half(half)
-            return s["iu"].at[(w,) + at + (rows,)]
+            return s["iu"].at[at + (pl.ds(0, SHARE), cols)]
 
         def four(k, half):
-            rows = pl.ds(0, SHARE) if half is None else rows_half(half)
             at = (pl.ds(0, 4), k % 4) if w == 0 else (k % 4, pl.ds(0, 4))
-            return s["iu"].at[(w,) + at + (rows,)]
+            return s["iu"].at[at + (pl.ds(0, SHARE), cols)]
 
         first, second = (along_x, along_y) if w == 0 else (along_y, along_x)
         yield from gather_direct(first, one, s["iu_sem"].at[w, 0])
@@ -388,12 +382,6 @@
             send(s["tu"].at[0, slots], s["tu"].at[1, slots], s["tc_sem"].at[part], other_core)
 
         yield from gather_eight(along_z, ref, sem, across)
-
-    def images_rings():
-        u = units(0)
-        for w in range(2):
-            s["iu"][w, 0, 0] = u[:, w * WIDE : (w + 1) * WIDE]
-        yield from together(images_ring(0), images_ring(1))
 
     def turned(t, t_ref, m_ref, n_ref):
         for k in range(1, 4):
@@ -411,38 +399,43 @@
         yield from turned(0, s["ti"], s["mi"], s["ni"])
         yield from turned(1, s["tt"], s["mt"], s["nt"])
 
-    interleave("ititti", t=texts_ring(), i=images_rings())
+    towers_task = towers()
+    interleave(
+        "tabwabtwatb",
+        t=texts_ring(),
+        a=images_ring(0),
+        b=images_ring(1),
+        w=(next(towers_task, None) for _ in range(2)),
+    )
 
     heat, shift = heat_ref[0], shift_ref[0]
     mult = cot_ref[0] * heat / 8192.0
 
-    def texts(n, w):
-        return s["tu"][n].reshape(256, EMB)[:, w * WIDE : (w + 1) * WIDE]
-
-    def images(w):
-        return s["iu"][w].reshape(512, WIDE)
+    def texts():
+        return s["tu"][...].reshape(512, EMB)
+
+    def images():
+        return s["iu"][...].reshape(512, EMB)
 
     def coefficients(n):
-        score = dot_nt(images(0), texts(n, 0)) + dot_nt(images(1), texts(n, 1))
+        score = dot_nt(images(), s["tu"][n].reshape(256, EMB))
         value = jax.nn.sigmoid(heat * score + shift)
         if n == 0:
             row = lax.broadcasted_iota(jnp.int32, (512, 256), 0)
             col = lax.broadcasted_iota(jnp.int32, (512, 256), 1)
             value = value - ((row == col) & (row < SHARE)).astype(F32)
-        s["coef"][n] = (mult * value).astype(BF16)
-
-    def text_half(n, w, out):
-        grad = dot_tn(s["coef"][n], images(w)).reshape(8, SHARE, WIDE)
-        out[:, :, w * WIDE : (w + 1) * WIDE] = grad.astype(out.dtype)
+        s["coef"][:, n * 256 : (n + 1) * 256] = (mult * value).astype(BF16)
+
+    def text_half(n, out):
+        grad = dot_tn(s["coef"][:, n * 256 : (n + 1) * 256], images())
+        out[...] = grad.reshape(8, SHARE, EMB).astype(out.dtype)
 
     coefficients(0)
     arrived(s["tu"].at[1, pl.ds(0, 5)], s["tc_sem"].at[0])
     arrived(s["tu"].at[1, pl.ds(5, 3)], s["tc_sem"].at[1])
     coefficients(1)
-    for w in range(2):
-        text_half(1, w, s["c_out"])
-        cols = pl.ds(w * WIDE, WIDE)
-        send(s["c_out"].at[:, :, cols], s["c_in"].at[:, :, cols], s["c_sem"].at[w], other_core)
+    text_half(1, s["c_out"])
+    send(s["c_out"], s["c_in"], s["c_sem"], other_core)
 
     def back(t, grads, grad):
         rs = s["rst"][t][:, :1]
@@ -451,11 +444,9 @@
         grads[0, 0, pl.ds(xh, 1)] = value.astype(BF16).reshape(1, SHARE, EMB)
 
     def text_grad():
-        for w in range(2):
-            text_half(0, w, s["own_t"])
-        for w in range(2):
-            cols = pl.ds(w * WIDE, WIDE)
-            arrived(s["c_in"].at[:, :, cols], s["c_sem"].at[w])
+        text_half(0, s["own_t"])
+        yield
+        arrived(s["c_in"], s["c_sem"])
 
         def own(k):
             at = AROUND.index(k)
@@ -466,7 +457,7 @@
         back(1, s["gt"], totals[0])
 
     def image_half(w):
-        grad = dot_nn(s["coef"][0], texts(0, w)) + dot_nn(s["coef"][1], texts(1, w))
+        grad = dot_nn(s["coef"][...], texts()[:, w * WIDE : (w + 1) * WIDE])
         s["own_i"][w] = grad.reshape(4, 4, SHARE, WIDE)
 
         def four(k):
@@ -486,10 +477,6 @@
             second, one, s["e2_out"].at[w], s["e2_in"].at[w], s["e2_sem"].at[w], totals
         )
         s["sum_i"][:, w * WIDE : (w + 1) * WIDE] = totals[0]
-
-    def image_grad():
-        yield from together(image_half(0), image_half(1))
-        back(0, s["gi"], s["sum_i"][...])
 
     def spread(t, grads, first_dot):
         def across(slots, h, n):
@@ -529,7 +516,7 @@
         for n, (h, slots) in enumerate(((xh, pl.ds(0, 4)), (ox, pl.ds(0, 3)), (ox, pl.ds(3, 1)))):
             arrived(grads.at[1, slots, h], s["gc_sem"].at[t, n])
 
-    def weights(t, grads, n_ref, p_ref, own, names, w_ref, out):
+    def weights(t, grads, n_ref, p_ref, own, names):
         def term(n):
             return dot_nn(n_ref[n], grads[n].reshape(256, EMB))
 
@@ -540,17 +527,26 @@
         p_ref[...] = p_ref[...] + term(1)
         totals = []
         ring = scatter_corner(t, own, names, totals)
-        chunks = [slice(k, k + CHUNK) for k in range(0, w_ref.shape[0], CHUNK)]
-        for _ in ring:
-            for cols in (chunks.pop(0),) if chunks else ():
-                value = dot_nt(grads[:, 0].reshape(ROWS, EMB), w_ref[cols, :]).astype(BF16)
-                for n, core in enumerate((co, oc)):
-                    for h in range(2):
-                        rows = pl.ds(pl.multiple_of((h * 2 + core) * SHARE, SHARE), SHARE)
-                        at = (n * 2 + h) * SHARE
-                        out[rows, cols] = value[at : at + SHARE]
+        yield from ring
+        return totals[0]
+
+    def inputs(grads, w_ref, out):
+        for k in range(0, w_ref.shape[0], CHUNK):
+            cols = slice(k, k + CHUNK)
+            value = dot_nt(grads[:, 0].reshape(ROWS, EMB), w_ref[cols, :]).astype(BF16)
+            for n, core in enumerate((co, oc)):
+                for h in range(2):
+                    rows = pl.ds(pl.multiple_of((h * 2 + core) * SHARE, SHARE), SHARE)
+                    at = (n * 2 + h) * SHARE
+                    out[rows, cols] = value[at : at + SHARE]
             yield
-        return totals[0]
+
+    def drain():
+        while True:
+            for _ in range(len(sends) - len(drained)):
+                drained.append(sends[len(drained)])
+                drained[-1].wait_send()
+            yield
 
     def own_i(k, half):
         n = half * 8 + lax.rem(z + 8 + k, 8)
@@ -563,17 +559,27 @@
 
     def texts_back():
         yield from text_grad()
-        op_t[...] = yield from weights(1, s["gt"], s["nt"], s["pt"], own_t, "ft", s["wt"], og_t)
+        op_t[...] = yield from weights(1, s["gt"], s["nt"], s["pt"], own_t, "ft")
 
     def images_back():
-        yield from image_grad()
-        total = yield from weights(0, s["gi"], s["ni"], s["pi"], own_i, "fi", s["wi"], og_i)
+        back(0, s["gi"], s["sum_i"][...])
+        total = yield from weights(0, s["gi"], s["ni"], s["pi"], own_i, "fi")
         op_i[:, :WIDE] = total[:OI]
         op_i[:, WIDE:] = total[OI:]
 
-    interleave("itwwtwititwitiititwitititit", i=images_back(), t=texts_back(), w=towers())
-    for copy in sends:
-        copy.wait_send()
+    drains = drain()
+    interleave(
+        "abttwatbabitwititiittiptiotoiptowxiopxt",
+        t=texts_back(),
+        a=image_half(0),
+        b=image_half(1),
+        i=images_back(),
+        w=towers_task,
+        o=inputs(s["gi"], s["wi"], og_i),
+        p=inputs(s["gt"], s["wt"], og_t),
+        x=(next(drains) for _ in range(2)),
+    )
+    next(drains)
 
 
 def per_device(xi, xt, wi, wt, heat, shift, cot):

time: 85 us -> 83.1 us (0.978)
  Pallas kernels: 77.2 us -> 75.7 us
    pallas_call x1, Pallas kernels: 77.2 us -> 75.7 us  [per_device(): pl.pallas_call(kernel, out_shape=shapes, in_specs=[hbm] * 4 + [smem] * 3,...]
where the time goes in v2:
time: 83.1 us; the launch traced here: 82.9 us
  Pallas kernels  75.7 us (91%)
  local copies, waits for them, and re-layouts  4.66 us (6%)
  between operations  2.59 us (3%)
    pallas_call x1, Pallas kernels, per_device(): pl.pallas_call(kernel, out_shape=shapes, in_specs=[hbm] * 4 + [smem] * 3,...  75.7 us
    unnamed x8, local copies, waits for them, and re-layouts  4.66 us

profile of v2, /device:TPU:2, one launch (start us, length us, event | category | flops | bytes accessed | tf_op | source)
XLA Modules:
  0.0 82.9 jit_solution(15431701677112178572)
XLA Ops:
  2.6 0.0 copy-start
  2.6 1.0 %copy-done = bf16[128,1536]{1,0:T(8,128)(2,1)S(1)} copy-done((bf16[128,1536]{1,0:T(8,128)(2,1)S(1)}, bf16[128,1536]{1,0:T(8,128)(2,1)}, u32[]{:S(2)}) %copy-start) | copy-done | bytes 393240
  3.6 0.0 copy-start.1
  3.6 0.9 %copy-done.1 = bf16[128,1024]{1,0:T(8,128)(2,1)S(1)} copy-done((bf16[128,1024]{1,0:T(8,128)(2,1)S(1)}, bf16[128,1024]{1,0:T(8,128)(2,1)}, u32[]{:S(2)}) %copy-start.1) | copy-done | bytes 262168
  4.5 75.7 %shard_map.102 = (bf16[128,1536]{1,0:T(8,128)(2,1)S(1)}, bf16[128,1024]{1,0:T(8,128)(2,1)S(1)}, f32[24,1024]{1,0:T(8,128)S(1)}, f32[16,1024]{1,0:T(8,128)S(1)}) custom-call(bf16[128,1536]{1,0:T(8,128)(2,1)S(1)} %copy-done, bf16[128,1024]{1,0:T(8,128)(2,1)S(1)} %copy-done.1, bf16[1536,1024]{1,0:T(8,128)(2,1)} %wi_h.1, bf16[1024,1024]{1,0:T(8,128)(2,1)} %wt_h.1, ...), custom_call_target="tpu_custom_call" | custom-call | tf_op jit(solution)/shard_map/pallas_call | solution.py:595
  80.2 0.7 copy.18
  80.9 0.7 copy.19
  81.6 0.6 copy.20
  82.3 0.6 copy.21
Async XLA Ops:
  2.6 1.0 %copy-start = (bf16[128,1536]{1,0:T(8,128)(2,1)S(1)}, bf16[128,1536]{1,0:T(8,128)(2,1)}, u32[]{:S(2)}) copy-start(bf16[128,1536]{1,0:T(8,128)(2,1)} %xi_h.1) | copy-start | bytes 1179652
  3.6 0.9 %copy-start.1 = (bf16[128,1024]{1,0:T(8,128)(2,1)S(1)}, bf16[128,1024]{1,0:T(8,128)(2,1)}, u32[]{:S(2)}) copy-start(bf16[128,1024]{1,0:T(8,128)(2,1)} %xt_h.1) | copy-start | bytes 786436

commit v3 on v2

--- a/solution.py
+++ b/solution.py
@@ -60,10 +60,8 @@
         own_t=v((8, SHARE, EMB), F32),
         d_out=v((4, 2, SHARE, EMB), BF16),
         d_in=v((4, 2, SHARE, EMB), BF16),
-        own_i=v((2, 4, 4, SHARE, WIDE), F32),
         e1_out=v((2, 4, 4, SHARE, WIDE), BF16),
         e1_in=v((2, 4, 4, SHARE, WIDE), BF16),
-        mid_i=v((2, 4, SHARE, WIDE), F32),
         e2_out=v((2, 4, SHARE, WIDE), BF16),
         e2_in=v((2, 4, SHARE, WIDE), BF16),
         sum_i=v((SHARE, EMB), F32),
@@ -231,13 +229,12 @@
         for k in (1, -1, 2):
             arrived(ref(k, None), sem.at[k % 4])
 
-    def scatter_direct(to, own, out, inn, sem, totals):
+    def scatter_direct(to, src, mine_, inn, sem, totals):
         for way in (2, 1, -1):
             k = -way % 4
-            out[k] = own(way).astype(BF16)
-            send(out.at[k], inn.at[k], sem.at[k], to[way])
-        value = own(0)
-        yield
+            send(src(way % 4), inn.at[k], sem.at[k], to[way])
+        yield
+        value = mine_()
         for k in (1, -1, 2):
             arrived(inn.at[k % 4], sem.at[k % 4])
             value = value + inn[k % 4].astype(F32)
@@ -457,26 +454,24 @@
         back(1, s["gt"], totals[0])
 
     def image_half(w):
+        first, second = (along_y, along_x) if w == 0 else (along_x, along_y)
+        out = s["e1_out"].at[w]
         grad = dot_nn(s["coef"][...], texts()[:, w * WIDE : (w + 1) * WIDE])
-        s["own_i"][w] = grad.reshape(4, 4, SHARE, WIDE)
-
-        def four(k):
-            return s["own_i"][0, :, k % 4] if w == 0 else s["own_i"][1, k % 4]
-
-        def one(k):
-            return s["mid_i"][w, k % 4]
-
-        first, second = (along_y, along_x) if w == 0 else (along_x, along_y)
+        out[...] = grad.astype(BF16).reshape(4, 4, SHARE, WIDE)
+
+        def group(k):
+            return out.at[:, k] if w == 0 else out.at[k]
+
         totals = []
         yield from scatter_direct(
-            first, four, s["e1_out"].at[w], s["e1_in"].at[w], s["e1_sem"].at[w], totals
+            first, group, lambda: group(0)[...].astype(F32), s["e1_in"].at[w], s["e1_sem"].at[w], totals
         )
-        s["mid_i"][w] = totals[0]
-        totals = []
+        line = s["e2_out"].at[w]
+        line[...] = totals[0].astype(BF16)
         yield from scatter_direct(
-            second, one, s["e2_out"].at[w], s["e2_in"].at[w], s["e2_sem"].at[w], totals
+            second, lambda k: line.at[k], lambda: totals[0][0], s["e2_in"].at[w], s["e2_sem"].at[w], totals
         )
-        s["sum_i"][:, w * WIDE : (w + 1) * WIDE] = totals[0]
+        s["sum_i"][:, w * WIDE : (w + 1) * WIDE] = totals[1]
 
     def spread(t, grads, first_dot):
         def across(slots, h, n):
@@ -599,7 +594,7 @@
         out_specs=[vmem] * 4,
         scratch_shapes=list(scratch().values()),
         compiler_params=pltpu.CompilerParams(
-            collective_id=0, has_side_effects=True, vmem_limit_bytes=52 * 1024 * 1024
+            collective_id=0, has_side_effects=True, vmem_limit_bytes=55_250_000
         ),
     )(xi, xt, wi, wt, heat, shift, cot)
 

time: 83.1 us -> 82 us (0.987)
  local copies, waits for them, and re-layouts: 4.66 us -> 3.66 us
    unnamed x8 -> x6, local copies, waits for them, and re-layouts: 4.66 us -> 3.66 us
where the time goes in v3:
time: 82 us; the launch traced here: 81.9 us
  Pallas kernels  75.6 us (92%)
  local copies, waits for them, and re-layouts  3.66 us (4%)
  between operations  2.59 us (3%)
    pallas_call x1, Pallas kernels, per_device(): pl.pallas_call(kernel, out_shape=shapes, in_specs=[hbm] * 4 + [smem] * 3,...  75.6 us
    unnamed x6, local copies, waits for them, and re-layouts  3.66 us

profile of v3, /device:TPU:2, one launch (start us, length us, event | category | flops | bytes accessed | tf_op | source)
XLA Modules:
  0.0 81.9 jit_solution(12716493986854634207)
XLA Ops:
  2.6 0.0 copy-start
  2.6 0.9 %copy-done = bf16[128,1024]{1,0:T(8,128)(2,1)S(1)} copy-done((bf16[128,1024]{1,0:T(8,128)(2,1)S(1)}, bf16[128,1024]{1,0:T(8,128)(2,1)}, u32[]{:S(2)}) %copy-start) | copy-done | bytes 262168
  3.5 75.6 %shard_map.102 = (bf16[128,1536]{1,0:T(8,128)(2,1)S(1)}, bf16[128,1024]{1,0:T(8,128)(2,1)S(1)}, f32[24,1024]{1,0:T(8,128)S(1)}, f32[16,1024]{1,0:T(8,128)S(1)}) custom-call(bf16[128,1536]{1,0:T(8,128)(2,1)} %xi_h.1, bf16[128,1024]{1,0:T(8,128)(2,1)S(1)} %copy-done, bf16[1536,1024]{1,0:T(8,128)(2,1)} %wi_h.1, bf16[1024,1024]{1,0:T(8,128)(2,1)} %wt_h.1, ...), custom_call_target="tpu_custom_call" | custom-call | tf_op jit(solution)/shard_map/pallas_call | solution.py:590
  79.2 0.7 copy.18
  79.9 0.7 copy.19
  80.6 0.6 copy.20
  81.3 0.6 copy.21
Async XLA Ops:
  2.6 1.0 %copy-start = (bf16[128,1024]{1,0:T(8,128)(2,1)S(1)}, bf16[128,1024]{1,0:T(8,128)(2,1)}, u32[]{:S(2)}) copy-start(bf16[128,1024]{1,0:T(8,128)(2,1)} %xt_h.1) | copy-start | bytes 786436

commit v4 on v3

--- a/solution.py
+++ b/solution.py
@@ -398,7 +398,7 @@
 
     towers_task = towers()
     interleave(
-        "tabwabtwatb",
+        "atbwwabtatb",
         t=texts_ring(),
         a=images_ring(0),
         b=images_ring(1),
@@ -564,7 +564,7 @@
 
     drains = drain()
     interleave(
-        "abttwatbabitwititiittiptiotoiptowxiopxt",
+        "battbtabaiwtititwititioptiotpoitwxixtop",
         t=texts_back(),
         a=image_half(0),
         b=image_half(1),

time: 82 us -> 83.7 us (1.021)
  Pallas kernels: 75.6 us -> 77.3 us
    pallas_call x1, Pallas kernels: 75.6 us -> 77.3 us  [per_device(): pl.pallas_call(kernel, out_shape=shapes, in_specs=[hbm] * 4 + [smem] * 3,...]
where the time goes in v4:
time: 83.7 us; the launch traced here: 83.6 us
  Pallas kernels  77.3 us (92%)
  local copies, waits for them, and re-layouts  3.66 us (4%)
  between operations  2.59 us (3%)
    pallas_call x1, Pallas kernels, per_device(): pl.pallas_call(kernel, out_shape=shapes, in_specs=[hbm] * 4 + [smem] * 3,...  77.3 us
    unnamed x6, local copies, waits for them, and re-layouts  3.66 us

profile of v4, /device:TPU:2, one launch (start us, length us, event | category | flops | bytes accessed | tf_op | source)
XLA Modules:
  0.0 83.6 jit_solution(1553262991945323367)
XLA Ops:
  2.6 0.0 copy-start
  2.6 0.9 %copy-done = bf16[128,1024]{1,0:T(8,128)(2,1)S(1)} copy-done((bf16[128,1024]{1,0:T(8,128)(2,1)S(1)}, bf16[128,1024]{1,0:T(8,128)(2,1)}, u32[]{:S(2)}) %copy-start) | copy-done | bytes 262168
  3.5 77.3 %shard_map.102 = (bf16[128,1536]{1,0:T(8,128)(2,1)S(1)}, bf16[128,1024]{1,0:T(8,128)(2,1)S(1)}, f32[24,1024]{1,0:T(8,128)S(1)}, f32[16,1024]{1,0:T(8,128)S(1)}) custom-call(bf16[128,1536]{1,0:T(8,128)(2,1)} %xi_h.1, bf16[128,1024]{1,0:T(8,128)(2,1)S(1)} %copy-done, bf16[1536,1024]{1,0:T(8,128)(2,1)} %wi_h.1, bf16[1024,1024]{1,0:T(8,128)(2,1)} %wt_h.1, ...), custom_call_target="tpu_custom_call" | custom-call | tf_op jit(solution)/shard_map/pallas_call | solution.py:590
  80.8 0.7 copy.18
  81.6 0.7 copy.19
  82.3 0.6 copy.20
  82.9 0.6 copy.21
Async XLA Ops:
  2.6 1.0 %copy-start = (bf16[128,1024]{1,0:T(8,128)(2,1)S(1)}, bf16[128,1024]{1,0:T(8,128)(2,1)}, u32[]{:S(2)}) copy-start(bf16[128,1024]{1,0:T(8,128)(2,1)} %xt_h.1) | copy-start | bytes 786436

commit v5 on v3

--- a/solution.py
+++ b/solution.py
@@ -83,7 +83,7 @@
         ft_in=v((2, 3, 2, OT, EMB), BF16),
         ft_end=v((2, 2, OT, EMB), BF16),
         ft_side=v((2, OT, EMB), BF16),
-        in_sem=dma((7,)),
+        in_sem=dma((5,)),
         x_sem=dma((2, 4)),
         a_sem=dma((2,)),
         b_sem=dma((2,)),
@@ -281,25 +281,25 @@
         copy.start()
         return copy
 
-    def load_rows(src, dst, k, n):
-        rows = pl.ds(k * CHUNK, CHUNK)
-        return load(src.at[rows], dst.at[rows], n)
+    def load_rows(src, dst, at, size, n):
+        rows = pl.ds(at, size)
+        return slice(at, at + size), load(src.at[rows], dst.at[rows], n)
 
     xi_load = load(xi_h, s["xi"], 0)
-    wi_loads = [load_rows(wi_h, s["wi"], k, 1 + k) for k in range(FI // CHUNK)]
-    xt_load = load(xt_h, s["xt"], 4)
-    wt_loads = [load_rows(wt_h, s["wt"], k, 5 + k) for k in range(FT // CHUNK)]
+    wi_loads = [load_rows(wi_h, s["wi"], 0, FI // 2, 1), load_rows(wi_h, s["wi"], FI // 2, FI // 2, 2)]
 
     barrier = pltpu.get_barrier_semaphore()
     peers = [other_core, *along_x.values(), *along_y.values(), *along_z.values(), *corners]
     for to in peers:
         pl.semaphore_signal(barrier, inc=1, device_id=to, device_id_type=MESH)
 
+    xt_load = load(xt_h, s["xt"], 3)
+    wt_loads = [load_rows(wt_h, s["wt"], 0, FT, 4)]
+
     def partial(t, x_ref, w_ref, x_load, w_loads):
         x_load.wait()
-        for k, w_load in enumerate(w_loads):
+        for k, (rows, w_load) in enumerate(w_loads):
             w_load.wait()
-            rows = slice(k * CHUNK, (k + 1) * CHUNK)
             part = dot_nn(x_ref[:, rows], w_ref[rows, :])
             s["part"][t] = part if k == 0 else s["part"][t] + part
             yield
@@ -417,11 +417,12 @@
     def coefficients(n):
         score = dot_nt(images(), s["tu"][n].reshape(256, EMB))
         value = jax.nn.sigmoid(heat * score + shift)
+        s["coef"][:, n * 256 : (n + 1) * 256] = (mult * value).astype(BF16)
         if n == 0:
-            row = lax.broadcasted_iota(jnp.int32, (512, 256), 0)
-            col = lax.broadcasted_iota(jnp.int32, (512, 256), 1)
-            value = value - ((row == col) & (row < SHARE)).astype(F32)
-        s["coef"][:, n * 256 : (n + 1) * 256] = (mult * value).astype(BF16)
+            row = lax.broadcasted_iota(jnp.int32, (SHARE, 128), 0)
+            col = lax.broadcasted_iota(jnp.int32, (SHARE, 128), 1)
+            own = value[:SHARE, :128] - (row == col).astype(F32)
+            s["coef"][:SHARE, :128] = (mult * own).astype(BF16)
 
     def text_half(n, out):
         grad = dot_tn(s["coef"][:, n * 256 : (n + 1) * 256], images())

time: 82 us -> 81.8 us (level)
  no operation moved by 1% of the time
where the time goes in v5:
time: 81.8 us; the launch traced here: 81.7 us
  Pallas kernels  75.4 us (92%)
  local copies, waits for them, and re-layouts  3.66 us (4%)
  between operations  2.59 us (3%)
    pallas_call x1, Pallas kernels, per_device(): pl.pallas_call(kernel, out_shape=shapes, in_specs=[hbm] * 4 + [smem] * 3,...  75.4 us
    unnamed x6, local copies, waits for them, and re-layouts  3.66 us

profile of v5, /device:TPU:2, one launch (start us, length us, event | category | flops | bytes accessed | tf_op | source)
XLA Modules:
  0.0 81.7 jit_solution(6298160050127241266)
XLA Ops:
  2.6 0.0 copy-start
  2.6 0.9 %copy-done = bf16[128,1024]{1,0:T(8,128)(2,1)S(1)} copy-done((bf16[128,1024]{1,0:T(8,128)(2,1)S(1)}, bf16[128,1024]{1,0:T(8,128)(2,1)}, u32[]{:S(2)}) %copy-start) | copy-done | bytes 262168
  3.5 75.4 %shard_map.102 = (bf16[128,1536]{1,0:T(8,128)(2,1)S(1)}, bf16[128,1024]{1,0:T(8,128)(2,1)S(1)}, f32[24,1024]{1,0:T(8,128)S(1)}, f32[16,1024]{1,0:T(8,128)S(1)}) custom-call(bf16[128,1536]{1,0:T(8,128)(2,1)} %xi_h.1, bf16[128,1024]{1,0:T(8,128)(2,1)S(1)} %copy-done, bf16[1536,1024]{1,0:T(8,128)(2,1)} %wi_h.1, bf16[1024,1024]{1,0:T(8,128)(2,1)} %wt_h.1, ...), custom_call_target="tpu_custom_call" | custom-call | tf_op jit(solution)/shard_map/pallas_call | solution.py:591
  79.0 0.7 copy.18
  79.7 0.7 copy.19
  80.4 0.6 copy.20
  81.1 0.6 copy.21
Async XLA Ops:
  2.6 1.0 %copy-start = (bf16[128,1024]{1,0:T(8,128)(2,1)S(1)}, bf16[128,1024]{1,0:T(8,128)(2,1)}, u32[]{:S(2)}) copy-start(bf16[128,1024]{1,0:T(8,128)(2,1)} %xt_h.1) | copy-start | bytes 786436

commit v6 on v5

--- a/solution.py
+++ b/solution.py
@@ -578,6 +578,14 @@
     next(drains)
 
 
+def copy_out(*refs):
+    copies = [pltpu.make_async_copy(refs[k], refs[4 + k], refs[8].at[k]) for k in range(4)]
+    for copy in copies:
+        copy.start()
+    for copy in copies:
+        copy.wait()
+
+
 def per_device(xi, xt, wi, wt, heat, shift, cot):
     vmem = pl.BlockSpec(memory_space=pltpu.VMEM)
     smem = pl.BlockSpec(memory_space=pltpu.SMEM)
@@ -588,7 +596,7 @@
         jax.ShapeDtypeStruct((OI, EMB), F32),
         jax.ShapeDtypeStruct((OT, EMB), F32),
     )
-    return pl.pallas_call(
+    outs = pl.pallas_call(
         kernel,
         out_shape=shapes,
         in_specs=[hbm] * 4 + [smem] * 3,
@@ -598,6 +606,14 @@
             collective_id=0, has_side_effects=True, vmem_limit_bytes=55_250_000
         ),
     )(xi, xt, wi, wt, heat, shift, cot)
+    return pl.pallas_call(
+        copy_out,
+        out_shape=shapes,
+        in_specs=[hbm] * 4,
+        out_specs=[hbm] * 4,
+        scratch_shapes=[pltpu.SemaphoreType.DMA((4,))],
+        compiler_params=pltpu.CompilerParams(vmem_limit_bytes=2 * 1024 * 1024),
+    )(*outs)
 
 
 def solution(mesh):

time: 81.8 us -> 80 us (0.978)
  local copies, waits for them, and re-layouts: 3.66 us -> 0.94 us
  Pallas kernels: 75.4 us -> 76.4 us
    unnamed x6 -> x2, local copies, waits for them, and re-layouts: 3.66 us -> 0.94 us
    pallas_call x0 -> x1, Pallas kernels: none -> 0.92 us  [per_device(): pl.pallas_call(copy_out, out_shape=shapes, in_specs=[hbm] * 4, out_specs=...]
where the time goes in v6:
time: 80 us; the launch traced here: 79.9 us
  Pallas kernels  76.4 us (96%)
  between operations  2.59 us (3%)
  local copies, waits for them, and re-layouts  0.94 us (1%)
    pallas_call x1, Pallas kernels, per_device(): pl.pallas_call(kernel, out_shape=shapes, in_specs=[hbm] * 4 + [smem] * 3,...  75.4 us

profile of v6, /device:TPU:2, one launch (start us, length us, event | category | flops | bytes accessed | tf_op | source)
XLA Modules:
  0.0 79.9 jit_solution(13214529632488301637)
XLA Ops:
  2.6 0.0 copy-start
  2.6 0.9 %copy-done = bf16[128,1024]{1,0:T(8,128)(2,1)S(1)} copy-done((bf16[128,1024]{1,0:T(8,128)(2,1)S(1)}, bf16[128,1024]{1,0:T(8,128)(2,1)}, u32[]{:S(2)}) %copy-start) | copy-done | bytes 262168
  3.5 75.4 %shard_map.102 = (bf16[128,1536]{1,0:T(8,128)(2,1)S(1)}, bf16[128,1024]{1,0:T(8,128)(2,1)S(1)}, f32[24,1024]{1,0:T(8,128)S(1)}, f32[16,1024]{1,0:T(8,128)S(1)}) custom-call(bf16[128,1536]{1,0:T(8,128)(2,1)} %xi_h.1, bf16[128,1024]{1,0:T(8,128)(2,1)S(1)} %copy-done, bf16[1536,1024]{1,0:T(8,128)(2,1)} %wi_h.1, bf16[1024,1024]{1,0:T(8,128)(2,1)} %wt_h.1, ...), custom_call_target="tpu_custom_call" | custom-call | tf_op jit(solution)/shard_map/pallas_call | solution.py:599
  79.0 0.9 %shard_map.103 = (bf16[128,1536]{1,0:T(8,128)(2,1)}, bf16[128,1024]{1,0:T(8,128)(2,1)}, f32[24,1024]{1,0:T(8,128)}, f32[16,1024]{1,0:T(8,128)}) custom-call(bf16[128,1536]{1,0:T(8,128)(2,1)S(1)} %get-tuple-element.8.refs_0_, bf16[128,1024]{1,0:T(8,128)(2,1)S(1)} %get-tuple-element.9.refs_1_, f32[24,1024]{1,0:T(8,128)S(1)} %get-tuple-element.10.refs_2_, ...), custom_call_target="tpu_custom_call" | custom-call | tf_op jit(solution)/shard_map/pallas_call | solution.py:609
Async XLA Ops:
  2.6 1.0 %copy-start = (bf16[128,1024]{1,0:T(8,128)(2,1)S(1)}, bf16[128,1024]{1,0:T(8,128)(2,1)}, u32[]{:S(2)}) copy-start(bf16[128,1024]{1,0:T(8,128)(2,1)} %xt_h.1) | copy-start | bytes 786436

commit v7 on v6

--- a/solution.py
+++ b/solution.py
@@ -121,7 +121,8 @@
         left = [task for task in left if next(task, True) is not True]
 
 
-def kernel(xi_h, xt_h, wi_h, wt_h, heat_ref, shift_ref, cot_ref, og_i, og_t, op_i, op_t, *refs):
+def kernel(xi_h, xt_h, wi_h, wt_h, heat_ref, shift_ref, cot_ref, *refs):
+    og_i, og_t, (op_i, op_t), refs = refs[:3], refs[3:5], refs[5:7], refs[7:]
     s = dict(zip(NAMES, refs))
     g = lax.axis_index("grp")
     b = lax.axis_index("blk")
@@ -534,7 +535,7 @@
                 for h in range(2):
                     rows = pl.ds(pl.multiple_of((h * 2 + core) * SHARE, SHARE), SHARE)
                     at = (n * 2 + h) * SHARE
-                    out[rows, cols] = value[at : at + SHARE]
+                    out[k // CHUNK][rows, :] = value[at : at + SHARE]
             yield
 
     def drain():
@@ -579,7 +580,11 @@
 
 
 def copy_out(*refs):
-    copies = [pltpu.make_async_copy(refs[k], refs[4 + k], refs[8].at[k]) for k in range(4)]
+    blocks, outs, sem = refs[:7], refs[7:11], refs[11]
+    places = [outs[0].at[:, pl.ds(k, CHUNK)] for k in range(0, FI, CHUNK)]
+    places += [outs[1].at[:, pl.ds(k, CHUNK)] for k in range(0, FT, CHUNK)]
+    places += outs[2:]
+    copies = [pltpu.make_async_copy(blocks[k], places[k], sem.at[k]) for k in range(7)]
     for copy in copies:
         copy.start()
     for copy in copies:
@@ -598,20 +603,20 @@
     )
     outs = pl.pallas_call(
         kernel,
-        out_shape=shapes,
+        out_shape=(jax.ShapeDtypeStruct((ROWS, CHUNK), BF16),) * 5 + shapes[2:],
         in_specs=[hbm] * 4 + [smem] * 3,
-        out_specs=[vmem] * 4,
+        out_specs=[vmem] * 7,
         scratch_shapes=list(scratch().values()),
         compiler_params=pltpu.CompilerParams(
-            collective_id=0, has_side_effects=True, vmem_limit_bytes=55_250_000
+            collective_id=0, has_side_effects=True, vmem_limit_bytes=55_600_000
         ),
     )(xi, xt, wi, wt, heat, shift, cot)
     return pl.pallas_call(
         copy_out,
         out_shape=shapes,
-        in_specs=[hbm] * 4,
+        in_specs=[hbm] * 7,
         out_specs=[hbm] * 4,
-        scratch_shapes=[pltpu.SemaphoreType.DMA((4,))],
+        scratch_shapes=[pltpu.SemaphoreType.DMA((7,))],
         compiler_params=pltpu.CompilerParams(vmem_limit_bytes=2 * 1024 * 1024),
     )(*outs)
 

time: 80 us -> 79.3 us (level)
  local copies, waits for them, and re-layouts: 0.94 us -> 0 us
    unnamed x2 -> x0, local copies, waits for them, and re-layouts: 0.94 us -> none
where the time goes in v7:
time: 79.3 us; the launch traced here: 79.1 us
  Pallas kernels  76.6 us (97%)
  between operations  2.58 us (3%)
    pallas_call x1, Pallas kernels, per_device(): pl.pallas_call(kernel, out_shape=(jax.ShapeDtypeStruct((ROWS, CHUNK), BF1...  75.6 us

profile of v7, /device:TPU:2, one launch (start us, length us, event | category | flops | bytes accessed | tf_op | source)
XLA Modules:
  0.0 79.1 jit_solution(228227978499400446)
XLA Ops:
  2.6 75.6 %shard_map.102 = (bf16[128,512]{1,0:T(8,128)(2,1)S(1)}, bf16[128,512]{1,0:T(8,128)(2,1)S(1)}, bf16[128,512]{1,0:T(8,128)(2,1)S(1)}, bf16[128,512]{1,0:T(8,128)(2...) custom-call(bf16[128,1536]{1,0:T(8,128)(2,1)} %xi_h.1, ...), custom_call_target="tpu_custom_call" | custom-call | tf_op jit(solution)/shard_map/pallas_call | solution.py:604
  78.2 0.9 %shard_map.103 = (bf16[128,1536]{1,0:T(8,128)(2,1)}, bf16[128,1024]{1,0:T(8,128)(2,1)}, f32[24,1024]{1,0:T(8,128)}, f32[16,1024]{1,0:T(8,128)}) custom-call(bf16[128,512]{1,0:T(8,128)(2,1)S(1)} %get-tuple-element.11.refs_0_, bf16[128,512]{1,0:T(8,128)(2,1)S(1)} %get-tuple-element.12.refs_1_, bf16[128,512]{1,0:T(8,128)(2,1)S(1)} %get-tuple-element.13.refs_2_, ...), custom_call_target="tpu_custom_call" | custom-call | tf_op jit(solution)/shard_map/pallas_call | solution.py:614

commit v8 on v7

--- a/solution.py
+++ b/solution.py
@@ -359,11 +359,12 @@
 
         def four(k, half):
             at = (pl.ds(0, 4), k % 4) if w == 0 else (k % 4, pl.ds(0, 4))
-            return s["iu"].at[at + (pl.ds(0, SHARE), cols)]
+            rows = pl.ds(0, SHARE) if half is None else rows_half(half)
+            return s["iu"].at[at + (rows, cols)]
 
         first, second = (along_x, along_y) if w == 0 else (along_y, along_x)
         yield from gather_direct(first, one, s["iu_sem"].at[w, 0])
-        yield from gather_direct(second, four, s["iu_sem"].at[w, 1])
+        yield from gather_four(second, four, s["iu_sem"].at[w, 1])
 
     def texts_ring():
         s["tu"][0, 0] = units(1)
@@ -399,7 +400,7 @@
 
     towers_task = towers()
     interleave(
-        "tabwabtwatb",
+        "tabwabtwabtab",
         t=texts_ring(),
         a=images_ring(0),
         b=images_ring(1),

time: 79.3 us -> 79.2 us (level)
  no operation moved by 1% of the time
where the time goes in v8:
time: 79.2 us; the launch traced here: 79.1 us
  Pallas kernels  76.5 us (97%)
  between operations  2.58 us (3%)
    pallas_call x1, Pallas kernels, per_device(): pl.pallas_call(kernel, out_shape=(jax.ShapeDtypeStruct((ROWS, CHUNK), BF1...  75.6 us

profile of v8, /device:TPU:2, one launch (start us, length us, event | category | flops | bytes accessed | tf_op | source)
XLA Modules:
  0.0 79.1 jit_solution(11172026464611807)
XLA Ops:
  2.6 75.6 %shard_map.102 = (bf16[128,512]{1,0:T(8,128)(2,1)S(1)}, bf16[128,512]{1,0:T(8,128)(2,1)S(1)}, bf16[128,512]{1,0:T(8,128)(2,1)S(1)}, bf16[128,512]{1,0:T(8,128)(2...) custom-call(bf16[128,1536]{1,0:T(8,128)(2,1)} %xi_h.1, ...), custom_call_target="tpu_custom_call" | custom-call | tf_op jit(solution)/shard_map/pallas_call | solution.py:605
  78.1 0.9 %shard_map.103 = (bf16[128,1536]{1,0:T(8,128)(2,1)}, bf16[128,1024]{1,0:T(8,128)(2,1)}, f32[24,1024]{1,0:T(8,128)}, f32[16,1024]{1,0:T(8,128)}) custom-call(bf16[128,512]{1,0:T(8,128)(2,1)S(1)} %get-tuple-element.11.refs_0_, bf16[128,512]{1,0:T(8,128)(2,1)S(1)} %get-tuple-element.12.refs_1_, bf16[128,512]{1,0:T(8,128)(2,1)S(1)} %get-tuple-element.13.refs_2_, ...), custom_call_target="tpu_custom_call" | custom-call | tf_op jit(solution)/shard_map/pallas_call | solution.py:615

commit v9 on v8

--- a/solution.py
+++ b/solution.py
@@ -241,6 +241,25 @@
             value = value + inn[k % 4].astype(F32)
         totals.append(value)
 
+    def scatter_four(to, src, inn, sem, totals):
+        for n, way in enumerate((1, -1)):
+            there = inn.at[2, pl.ds(0, 4), rows_half(n)]
+            send(src(2, rows_half(n)), there, sem.at[2 * n], to[way])
+        yield
+        for n, way in enumerate((1, -1)):
+            there = inn.at[2, pl.ds(0, 4), rows_half(n)]
+            arrived(there, sem.at[2 * n])
+            part = src(way % 4, rows_half(n))
+            part[...] = (part[...].astype(F32) + there[...].astype(F32)).astype(BF16)
+            k = -way % 4
+            send(src(way % 4, pl.ds(0, SHARE)), inn.at[k], sem.at[k], to[way])
+        yield
+        value = src(0, pl.ds(0, SHARE))[...].astype(F32)
+        for k in (3, 1):
+            arrived(inn.at[k], sem.at[k])
+            value = value + inn[k].astype(F32)
+        totals.append(value)
+
     def scatter_corner(t, own, name, totals):
         out, inn, end, side = (s[name + part] for part in ("_out", "_in", "_end", "_side"))
         sem, end_sem = s["f_sem"].at[t], s["end_sem"].at[t]
@@ -462,13 +481,11 @@
         grad = dot_nn(s["coef"][...], texts()[:, w * WIDE : (w + 1) * WIDE])
         out[...] = grad.astype(BF16).reshape(4, 4, SHARE, WIDE)
 
-        def group(k):
-            return out.at[:, k] if w == 0 else out.at[k]
+        def group(k, rows):
+            return out.at[pl.ds(0, 4), k, rows] if w == 0 else out.at[k, pl.ds(0, 4), rows]
 
         totals = []
-        yield from scatter_direct(
-            first, group, lambda: group(0)[...].astype(F32), s["e1_in"].at[w], s["e1_sem"].at[w], totals
-        )
+        yield from scatter_four(first, group, s["e1_in"].at[w], s["e1_sem"].at[w], totals)
         line = s["e2_out"].at[w]
         line[...] = totals[0].astype(BF16)
         yield from scatter_direct(
@@ -567,7 +584,7 @@
 
     drains = drain()
     interleave(
-        "abttwatbabitwititiittiptiotoiptowxiopxt",
+        "abttwabtababitwititiittiptiotoiptowxiopxt",
         t=texts_back(),
         a=image_half(0),
         b=image_half(1),

time: 79.2 us -> 81.4 us (1.028)
  Pallas kernels: 76.5 us -> 78.8 us
    pallas_call x1, Pallas kernels: 75.6 us -> 77.8 us  [per_device(): pl.pallas_call(kernel, out_shape=(jax.ShapeDtypeStruct((ROWS, CHUNK), BF1...]
where the time goes in v9:
time: 81.4 us; the launch traced here: 81.3 us
  Pallas kernels  78.8 us (97%)
  between operations  2.58 us (3%)
    pallas_call x1, Pallas kernels, per_device(): pl.pallas_call(kernel, out_shape=(jax.ShapeDtypeStruct((ROWS, CHUNK), BF1...  77.8 us

profile of v9, /device:TPU:2, one launch (start us, length us, event | category | flops | bytes accessed | tf_op | source)
XLA Modules:
  0.0 81.3 jit_solution(825864370209640424)
XLA Ops:
  2.6 77.8 %shard_map.102 = (bf16[128,512]{1,0:T(8,128)(2,1)S(1)}, bf16[128,512]{1,0:T(8,128)(2,1)S(1)}, bf16[128,512]{1,0:T(8,128)(2,1)S(1)}, bf16[128,512]{1,0:T(8,128)(2...) custom-call(bf16[128,1536]{1,0:T(8,128)(2,1)} %xi_h.1, ...), custom_call_target="tpu_custom_call" | custom-call | tf_op jit(solution)/shard_map/pallas_call | solution.py:622
  80.4 0.9 %shard_map.103 = (bf16[128,1536]{1,0:T(8,128)(2,1)}, bf16[128,1024]{1,0:T(8,128)(2,1)}, f32[24,1024]{1,0:T(8,128)}, f32[16,1024]{1,0:T(8,128)}) custom-call(bf16[128,512]{1,0:T(8,128)(2,1)S(1)} %get-tuple-element.11.refs_0_, bf16[128,512]{1,0:T(8,128)(2,1)S(1)} %get-tuple-element.12.refs_1_, bf16[128,512]{1,0:T(8,128)(2,1)S(1)} %get-tuple-element.13.refs_2_, ...), custom_call_target="tpu_custom_call" | custom-call | tf_op jit(solution)/shard_map/pallas_call | solution.py:632
